TPU v7x, 128 devices: a whole 4x4x4 slice. The times are simulated.
128 devices in a mesh: row: 8 (over x, y_lo), col: 16 (over y_hi, z, core).
Axes of the slice: x: 4, y: 4 (y_hi: 2, y_lo: 2; y = y_hi * 2 + y_lo), z: 4, core: 2. Of those that a mesh axis runs over, the one named last changes fastest.
Arguments:
- front: float32 [10240, 10240], P('row', 'col'), as said below
- updates: float32 [16384, 8192], P('row', 'col'), as said below
- maps: int32 [2, 64], replicated, may hold values from 0 to 79, as said below
Outputs:
- panel_factor: float32 [10240, 2048], P('row', 'col')
- trailing: float32 [10240, 10240], P('row', 'col')
Inputs may be any that keep to these rules, and one draw needn't show every extreme that they name: `maps`: each row lists 64 distinct front blocks; entry j leaves remainder floor(j / 4) on division by 16, the entries of one remainder rise with j, and blocks 0 and 79 appear in both rows. Symmetric in front order; the assembled leading 2048 x 2048 block is positive definite. `updates`: each child's update is symmetric in the child's own order.
All inputs are finite; a program needn't handle non-finite values.
Results may differ from a plain program's by a relative error of at most 0.0001.
Values sent between devices are 32-bit elements; how exact they have to be, the bound alone decides.
No kernel may reach another device: no remote copies, remote signals or barrier semaphores. Data moves between devices by JAX's collectives and lax.ppermute only.
A program may use at most 192 MiB of HBM per device.

v0:
```python
import jax
import jax.numpy as jnp
from jax import lax
from jax.sharding import PartitionSpec as P

BLK = 128
PW = 2048


def from_root(value, axis, source):
    kept = jnp.where(lax.axis_index(axis) == source, value, 0).astype(value.dtype)
    return lax.psum(kept, axis)


def block_cholesky(leading):
    order = leading.shape[0]
    count = order // BLK
    identity = jnp.eye(BLK, dtype=jnp.float32)
    factor = jnp.zeros((order, order), jnp.float32)
    inverses = []
    for step in range(count):
        start = step * BLK
        column = leading[start:, start : start + BLK]
        if step > 0:
            column = column - jnp.dot(
                factor[start:, :start],
                factor[start : start + BLK, :start].T,
                precision=lax.Precision.HIGHEST,
                preferred_element_type=jnp.float32,
            )
        diag_factor = jnp.linalg.cholesky(column[:BLK])
        inverse = jax.scipy.linalg.solve_triangular(diag_factor, identity, lower=True)
        inverses.append(inverse)
        factor = factor.at[start : start + BLK, start : start + BLK].set(diag_factor)
        if start + BLK < order:
            below = jnp.dot(
                column[BLK:],
                inverse.T,
                precision=lax.Precision.HIGHEST,
                preferred_element_type=jnp.float32,
            )
            factor = factor.at[start + BLK :, start : start + BLK].set(below)
    return (factor, inverses)


def block_solve(factor, inverses, rows_in):
    count = len(inverses)
    result = jnp.zeros(rows_in.shape, jnp.float32)
    for step in range(count):
        start = step * BLK
        target = rows_in[:, start : start + BLK]
        if step > 0:
            target = target - jnp.dot(
                result[:, :start],
                factor[start : start + BLK, :start].T,
                precision=lax.Precision.HIGHEST,
                preferred_element_type=jnp.float32,
            )
        solved = jnp.dot(
            target,
            inverses[step].T,
            precision=lax.Precision.HIGHEST,
            preferred_element_type=jnp.float32,
        )
        result = result.at[:, start : start + BLK].set(solved)
    return result


def local(front, updates, maps):
    rows_n = lax.axis_size("row")
    cols_n = lax.axis_size("col")
    half_rows = rows_n // 2
    row_at = lax.axis_index("row")
    col_at = lax.axis_index("col")
    front_rows, front_cols = front.shape
    row_slots = front_rows // BLK
    col_slots = front_cols // BLK
    col_group = updates.shape[1] // BLK
    depth_slots = col_group // half_rows
    width_slots = cols_n // rows_n
    child_blocks = maps.shape[1]
    outgoing = updates.reshape(width_slots, rows_n, depth_slots * BLK, col_group * BLK)
    incoming = lax.all_to_all(outgoing, "row", split_axis=1, concat_axis=1, tiled=True)
    incoming = incoming.reshape(width_slots, 2, half_rows, depth_slots, BLK, col_group, BLK)
    shape_grid = (width_slots, half_rows, depth_slots)
    grid_w = lax.broadcasted_iota(jnp.int32, shape_grid, 0)
    grid_a = lax.broadcasted_iota(jnp.int32, shape_grid, 1)
    grid_e = lax.broadcasted_iota(jnp.int32, shape_grid, 2)
    block_id = (((grid_w * rows_n + row_at) * depth_slots + grid_e) * half_rows + grid_a).reshape(
        -1
    )
    child_iota = jnp.arange(child_blocks, dtype=jnp.int32)
    assembled = front
    for which_child in range(2):
        child_map = maps[which_child]
        blocks = incoming[:, which_child].reshape(
            width_slots * half_rows * depth_slots, BLK, col_group, BLK
        )
        matched = block_id[:, None] == child_iota[None, :]
        targets = jnp.sum(jnp.where(matched, child_map[None, :], 0), axis=1)
        row_place = (
            targets[None, :] // rows_n == jnp.arange(row_slots, dtype=jnp.int32)[:, None]
        ).astype(jnp.float32)
        col_ids = lax.dynamic_slice_in_dim(child_map, col_at * col_group, col_group)
        col_place = (
            col_ids[None, :] // cols_n == jnp.arange(col_slots, dtype=jnp.int32)[:, None]
        ).astype(jnp.float32)
        placed = jnp.einsum("pn,nxvy->pxvy", row_place, blocks, precision=lax.Precision.HIGHEST)
        placed = jnp.einsum("pxvy,qv->pxqy", placed, col_place, precision=lax.Precision.HIGHEST)
        assembled = assembled + placed.reshape(front_rows, front_cols)
    panel_rslots = PW // BLK // rows_n
    panel_cslots = PW // BLK // cols_n
    gathered = lax.all_gather(assembled[:, : panel_cslots * BLK], "col", axis=1, tiled=True)
    panel_rows = (
        gathered.reshape(front_rows, cols_n, panel_cslots, BLK)
        .transpose(0, 2, 1, 3)
        .reshape(front_rows, PW)
    )
    corner = assembled[: panel_rslots * BLK, : panel_cslots * BLK]
    pieces = lax.all_gather(corner, ("row", "col"), axis=0, tiled=True)
    leading = (
        pieces.reshape(rows_n, cols_n, panel_rslots, BLK, panel_cslots, BLK)
        .transpose(2, 0, 3, 4, 1, 5)
        .reshape(PW, PW)
    )
    factor, inverses = block_cholesky(leading)
    lower_rows = block_solve(factor, inverses, panel_rows[panel_rslots * BLK :])
    head_rows = lax.dynamic_index_in_dim(
        factor.reshape(panel_rslots, rows_n, BLK, PW), row_at, 1, keepdims=False
    )
    factor_rows = jnp.concatenate([head_rows.reshape(panel_rslots * BLK, PW), lower_rows], axis=0)
    col_span = cols_n // rows_n
    root_row = col_at % rows_n
    picked = lax.dynamic_index_in_dim(
        factor_rows.reshape(col_slots, col_span, BLK, PW), col_at // rows_n, 1, keepdims=False
    )
    column_rows = from_root(picked.reshape(col_slots * BLK, PW), "row", root_row)
    update = jnp.dot(
        factor_rows,
        column_rows.T,
        precision=lax.Precision.HIGHEST,
        preferred_element_type=jnp.float32,
    )
    row_keep = jnp.arange(front_rows) // BLK >= panel_rslots
    col_keep = jnp.arange(front_cols) // BLK >= panel_cslots
    trailing = jnp.where(
        row_keep[:, None] & col_keep[None, :], assembled - update, jnp.float32(0.0)
    )
    panel_out = lax.dynamic_index_in_dim(
        factor_rows.reshape(front_rows, panel_cslots, cols_n, BLK), col_at, 2, keepdims=False
    )
    return (panel_out.reshape(front_rows, panel_cslots * BLK), trailing)


def solution(mesh):
    in_specs = (P("row", "col"), P("row", "col"), P())
    out_specs = (P("row", "col"), P("row", "col"))
    return jax.shard_map(local, mesh=mesh, in_specs=in_specs, out_specs=out_specs, check_vma=False)
```

profile of v0, /device:TPU:1, one launch (start us, length us, event | category | flops | bytes accessed | tf_op | source)
XLA Modules:
  0.0 1348.0 jit_solution(4815525074434272048)
XLA Ops:
  11.9 5.9 all-to-all-start
  18.3 58.4 %all-to-all-done = f32[2,8,128,512]{3,2,0,1:T(8,128)} async-done(((f32[2,8,128,512]{3,2,0,1:T(8,128)}), f32[2,8,128,512]{3,2,0,1:T(8,128)}, u32[]{:S(2)}, u32[]{:S(2)}) %all-to-all-start) | async-done | bytes 4194336 | tf_op jit(solution)/shard_map/all_to_all | solution.py:83
  108.5 208.8 %all-gather.3.cloned.1.call-done = f32[32768,128]{1,0:T(8,128)} async-done(((f32[256,128]{1,0:T(8,128)}), f32[32768,128]{1,0:T(8,128)}) %all-gather.3.cloned.1.call-update) | async-done | bytes 16777232 | tf_op jit(solution)/shard_map/all_gather | solution.py:120
  317.3 17.8 %copy.161 = f32[8,16,2,128,1,128]{3,0,2,5,1,4:T(8,128)} copy(f32[8,16,2,128,1,128]{5,3,2,1,0,4:T(8,128)} %bitcast.269) | data formatting | bytes 33554432 | tf_op jit(solution)/shard_map/reshape | solution.py:122
  335.1 18.0 %reshape.1456 = f32[2048,2048]{0,1:T(8,128)} reshape(f32[2,8,128,1,16,128]{2,1,0,5,4,3:T(8,128)} %bitcast.263) | data formatting | bytes 33554432 | tf_op jit(solution)/shard_map/reshape | solution.py:124
  354.9 11.7 cholesky.254
  368.0 9.8 custom-call.20
  378.1 7.8 scatter.156
  392.2 11.9 cholesky.265
  406.1 9.8 custom-call.21
  422.7 11.7 cholesky.276
  436.4 10.0 custom-call.22
  454.1 11.7 cholesky.287
  467.8 9.8 custom-call.23
  480.7 5.5 fusion.59
  486.3 11.7 cholesky.298
  500.0 9.8 custom-call.24
  512.4 5.9 fusion.56
  518.4 11.7 cholesky.309
  532.2 9.8 custom-call.25
  544.3 6.7 fusion.53
  551.2 11.7 cholesky.320
  564.9 9.8 custom-call.26
  576.9 6.6 fusion.50
  583.7 12.1 cholesky.331
  597.8 9.8 custom-call.27
  609.8 6.9 fusion.84
  616.8 11.9 cholesky.342
  630.6 9.8 custom-call.28
  642.4 6.3 fusion.128
  648.9 11.9 cholesky.353
  662.8 9.8 custom-call.29
  674.5 6.4 fusion.131
  681.0 11.7 cholesky.364
  694.7 10.2 custom-call.30
  706.6 5.9 fusion.134
  712.6 11.7 cholesky.375
  726.3 9.8 custom-call.31
  737.7 5.6 fusion.137
  743.5 11.7 cholesky.386
  757.2 9.8 custom-call.32
  773.1 11.9 cholesky.397
  787.0 9.8 custom-call.33
  802.0 11.7 cholesky.408
  815.7 10.2 custom-call.34
  829.8 11.7 cholesky.419
  850.1 9.8 custom-call.35
  891.2 6.5 fusion.93
  901.0 7.2 fusion.81
  911.2 8.5 fusion.116
  922.8 8.5 fusion.87
  934.4 9.7 fusion.119
  947.1 10.5 fusion.96
  960.8 11.5 fusion.122
  975.4 12.6 fusion.72
  991.0 13.4 fusion.75
  1007.5 14.3 %fusion.125 = f32[1024,128]{1,0:T(8,128)S(1)} fusion(f32[1024,2048]{0,1:T(8,128)} %fusion.100, f32[2048,2048]{1,0:T(8,128)} %get-tuple-element.575, f32[1280,2048]{1,0:T(8,128)S(1)} %bitcast.274), kind=kOutput, calls=%fused_computation.126 | convolution fusion | flops 2818703360 | bytes 9306112 | tf_op jit(solution)/shard_map/dot_general | solution.py:53
  1023.3 14.4 %fusion.78 = f32[1024,128]{1,0:T(8,128)S(1)} fusion(f32[1024,2048]{0,1:T(8,128)S(1)} %fusion.99, f32[2048,2048]{1,0:T(8,128)} %get-tuple-element.575, f32[1280,2048]{1,0:T(8,128)S(1)} %bitcast.274), kind=kOutput, calls=%fused_computation.84 | convolution fusion | flops 3020029952 | bytes 9895936 | tf_op jit(solution)/shard_map/dot_general | solution.py:53
  1041.6 6.5 pad_maximum_fusion
  1048.1 13.3 reshape.1460
  1061.3 21.0 %fusion.10 = f32[5,128,2048]{1,0,2:T(8,128)} fusion(pred[]{:T(512)S(6)} %eq.132, f32[5,2,128,2048]{2,1,0,3:T(2,128)} %reshape.1460, s32[]{:T(128)S(6)} %select_n.110), kind=kLoop, calls=%fused_computation.14 | loop fusion | flops 1310720 | bytes 10485765 | tf_op jit(solution)/shard_map/jit(_where)/select_n | solution.py:11
  1082.3 7.2 copy.231
  1098.3 211.5 %all-reduce.4.cloned.1.call-done = f32[640,2048]{0,1:T(8,128)} async-done(((f32[640,2048]{0,1:T(8,128)}), f32[640,2048]{0,1:T(8,128)}) %all-reduce.4.cloned.1.call-update) | async-done | bytes 5242896 | tf_op jit(solution)/shard_map/psum | solution.py:12
  1309.8 31.6 %fusion.33 = f32[1280,640]{1,0:T(8,128)} fusion(f32[1280,640]{1,0:T(8,128)} %copy-done.5, f32[640,2048]{0,1:T(8,128)} %all-reduce.4.cloned.1.call-done, pred[640]{0:T(1024)(128)(4,1)S(1)} %fusion.278, pred[1280]{0:T(1024)(128)(4,1)S(1)} %fusion.274, f32[1024,2048]{0,1:T(8,128)} %copy-done.1, f32[256,2048]{0,1:T(8,128)S(1)} %copy-done.4), kind=kOutput, calls=%fused_computation.39 | convolution fusion | flops 20137738240 | bytes 22284160 | tf_op jit(solution)/shard_map/dot_general | solution.py:138
  (220 shorter events, 206.2 us)
Async XLA Ops:
  7.2 10.9 copy-start.8
  11.9 64.8 %all-to-all-start = ((f32[2,8,128,512]{3,2,0,1:T(8,128)}), f32[2,8,128,512]{3,2,0,1:T(8,128)}, u32[]{:S(2)}, u32[]{:S(2)}) async-start(f32[2,8,128,512]{3,2,0,1:T(8,128)} %copy.156), calls=%async_computation | async-start | bytes 8388608 | tf_op jit(solution)/shard_map/all_to_all | solution.py:83
  17.8 299.5 %all-gather.3.cloned.1.call-start = ((), (), s32[]{:S(2)}) async-start(), calls=%async_computation.1 | async-start | bytes 16908288 | tf_op jit(solution)/shard_map/all_gather | solution.py:120
  89.3 9.9 copy-start.6
  101.1 234.0 %copy-start.5 = (f32[1280,640]{1,0:T(8,128)}, f32[1280,640]{1,0:T(8,128)S(1)}, u32[]{:S(2)}) copy-start(f32[1280,640]{1,0:T(8,128)S(1)} %bitcast_add_fusion) | copy-start | bytes 9830404
  101.8 741.7 %all-gather.5.cloned.1.call-start = ((), (), s32[]{:S(2)}) async-start(), calls=%async_computation.2 | async-start | bytes 11141120 | tf_op jit(solution)/shard_map/all_gather | solution.py:113
  108.5 1201.3 %all-reduce.4.cloned.1.call-start = ((), (), s32[]{:S(2)}) async-start(), calls=%async_computation.3 | async-start | bytes 10485760 | tf_op jit(solution)/shard_map/psum | solution.py:12
  862.6 35.1 %copy-start.2 = (f32[2,1,128,2048]{3,2,1,0:T(8,128)}, f32[2,1,128,2048]{3,2,1,0:T(8,128)S(1)}, u32[]{:S(2)}) copy-start(f32[2,1,128,2048]{3,2,1,0:T(8,128)S(1)} %constant_dynamic-slice_fusion) | copy-start | bytes 6291460
  875.3 35.9 %slice-start = ((s8[10485760]{0:T(1024)(128)(4,1)}), s8[4194304]{0:T(1024)(128)(4,1)S(1)}, s32[]{:S(2)}) async-start(s8[10485760]{0:T(1024)(128)(4,1)} %bitcast.273), calls=%async_computation.4 | async-start | bytes 8388608
  882.8 28.3 %slice-start.1 = ((s8[10485760]{0:T(1024)(128)(4,1)}), s8[4194304]{0:T(1024)(128)(4,1)S(1)}, s32[]{:S(2)}) async-start(s8[10485760]{0:T(1024)(128)(4,1)} %bitcast.273), calls=%async_computation.5 | async-start | bytes 8388608
  897.7 13.4 slice-start.2
  1007.5 14.4 %copy-start = (f32[1024,2048]{0,1:T(8,128)S(1)}, f32[1024,2048]{0,1:T(8,128)}, u32[]{:S(2)}) copy-start(f32[1024,2048]{0,1:T(8,128)} %fusion.100) | copy-start | bytes 25165828
  1021.8 15.9 %copy-start.7 = (f32[128,128]{1,0:T(8,128)S(1)}, f32[128,128]{1,0:T(8,128)}, u32[]{:S(2)}) copy-start(f32[128,128]{1,0:T(8,128)} %fusion.177) | copy-start | bytes 196612
  1038.3 3.3 copy-start.1
  1082.3 7.2 copy-start.3
  1093.0 216.8 %copy-start.4 = (f32[256,2048]{0,1:T(8,128)S(1)}, f32[256,2048]{0,1:T(8,128)}, u32[]{:S(2)}) copy-start(f32[256,2048]{0,1:T(8,128)} %copy.216) | copy-start | bytes 6291460
Sparse Core Ops, SparseCore 0:
  102.0 215.3 all-gather.2
  320.2 87.1 all-gather.4
  1089.6 220.1 all-reduce.3
where the time goes:
time: 1360 us; the launch traced here: 1350 us
  waiting for transfers between devices  479 us (35%)
  other arithmetic  415 us (31%)
  matrix products  331 us (24%)
  local copies, waits for them, and re-layouts  102 us (8%)
  between operations  15 us (1%)
    psum x1, waiting for transfers between devices, from_root(): return lax.psum(kept, axis)  211 us
    all_gather x1, waiting for transfers between devices, local(): pieces = lax.all_gather(corner, ('row', 'col'), axis=0, tiled=True)  209 us
    another operation x48, other arithmetic, block_cholesky(): diag_factor = jnp.linalg.cholesky(column[:BLK])  200 us
    another operation x32, other arithmetic, block_cholesky(): jax.scipy.linalg.solve_triangular(diag_factor, identity, lower=True)  178 us
    dot_general x15, matrix products, block_solve(): jnp.dot(result[:, :start], factor[start:start + BLK, :start].T, precision...  132 us
    dot_general x15, matrix products, block_cholesky(): jnp.dot(factor[start:, :start], factor[start:start + BLK, :start].T, prec...  77.6 us
    all_to_all x1, waiting for transfers between devices, local(): lax.all_to_all(outgoing, 'row', split_axis=1, concat_axis=1, tiled=True)  58.4 us
    dot_general x16, matrix products, block_solve(): jnp.dot(target, inverses[step].T, precision=lax.Precision.HIGHEST, prefer...  43.4 us
  transfers between devices with their start and end apart: 4, of which 3 were waited for; matrix products, arithmetic and copies ran while one was open for 40% of the time, Pallas kernels for 0%

commit v1 on v0

--- a/solution.py
+++ b/solution.py
@@ -117,7 +117,10 @@
         .reshape(front_rows, PW)
     )
     corner = assembled[: panel_rslots * BLK, : panel_cslots * BLK]
-    pieces = lax.all_gather(corner, ("row", "col"), axis=0, tiled=True)
+    pieces = jnp.concatenate(
+        lax.all_to_all(jnp.stack([corner] * lax.axis_size(("row", "col"))), ("row", "col"), 0, 0),
+        axis=0,
+    )
     leading = (
         pieces.reshape(rows_n, cols_n, panel_rslots, BLK, panel_cslots, BLK)
         .transpose(2, 0, 3, 4, 1, 5)

time: 1360 us -> 1370 us (level)
  matrix products: 331 us -> 298 us
  waiting for transfers between devices: 479 us -> 511 us
    all_to_all x0 -> x1, waiting for transfers between devices: none -> 231 us  [local(): lax.all_to_all(jnp.stack([corner] * lax.axis_size(('row', 'col'))), ('row...]
    all_gather x1 -> x0, waiting for transfers between devices: 209 us -> none  [local(): pieces = lax.all_gather(corner, ('row', 'col'), axis=0, tiled=True)]
    dot_general x16, matrix products: 43.4 us -> 22.1 us  [block_solve(): jnp.dot(target, inverses[step].T, precision=lax.Precision.HIGHEST, prefer...]
    reshape x1 -> x0, local copies, waits for them, and re-layouts: 17.8 us -> none  [local(): pieces.reshape(rows_n, cols_n, panel_rslots, BLK, panel_cslots, BLK)]
    transpose x0 -> x1, local copies, waits for them, and re-layouts: none -> 17.7 us  [local(): leading = pieces.reshape(rows_n, cols_n, panel_rslots, BLK, panel_cslots,...]
  transfers between devices with their start and end apart: 4 -> 4, of which waited for: 3 -> 3; matrix products, arithmetic and copies ran while one was open for 40% -> 41% of each run, Pallas kernels for 0% -> 0%
where the time goes in v1:
time: 1370 us; the launch traced here: 1360 us
  waiting for transfers between devices  511 us (37%)
  other arithmetic  415 us (30%)
  matrix products  298 us (22%)
  local copies, waits for them, and re-layouts  107 us (8%)
  starting transfers between devices  16.3 us (1%)
  between operations  15.6 us (1%)
    all_to_all x1, waiting for transfers between devices, local(): lax.all_to_all(jnp.stack([corner] * lax.axis_size(('row', 'col'))), ('row...  231 us
    psum x1, waiting for transfers between devices, from_root(): return lax.psum(kept, axis)  221 us
    another operation x48, other arithmetic, block_cholesky(): diag_factor = jnp.linalg.cholesky(column[:BLK])  200 us
    another operation x32, other arithmetic, block_cholesky(): jax.scipy.linalg.solve_triangular(diag_factor, identity, lower=True)  178 us
    dot_general x15, matrix products, block_solve(): jnp.dot(result[:, :start], factor[start:start + BLK, :start].T, precision...  122 us
    dot_general x15, matrix products, block_cholesky(): jnp.dot(factor[start:, :start], factor[start:start + BLK, :start].T, prec...  77.6 us
    all_to_all x1, waiting for transfers between devices, local(): lax.all_to_all(outgoing, 'row', split_axis=1, concat_axis=1, tiled=True)  58.5 us
    dot_general x1, matrix products, local(): jnp.dot(factor_rows, column_rows.T, precision=lax.Precision.HIGHEST, pref...  31.4 us
  transfers between devices with their start and end apart: 4, of which 3 were waited for; matrix products, arithmetic and copies ran while one was open for 41% of the time, Pallas kernels for 0%

profile of v1, /device:TPU:1, one launch (start us, length us, event | category | flops | bytes accessed | tf_op | source)
XLA Modules:
  0.0 1363.2 jit_solution(4588088179376667469)
XLA Ops:
  11.9 5.9 all-to-all-start
  18.3 58.5 %all-to-all-done = f32[2,8,128,512]{3,2,0,1:T(8,128)} async-done(((f32[2,8,128,512]{3,2,0,1:T(8,128)}), f32[2,8,128,512]{3,2,0,1:T(8,128)}, u32[]{:S(2)}, u32[]{:S(2)}) %all-to-all-start) | async-done | bytes 4194336 | tf_op jit(solution)/shard_map/all_to_all | solution.py:83
  100.9 7.8 stack.2
  108.7 10.3 all-to-all-start.1
  125.5 230.8 %all-to-all-done.1 = f32[128,256,128]{2,1,0:T(8,128)} async-done(((f32[128,256,128]{2,1,0:T(8,128)}), f32[128,256,128]{2,1,0:T(8,128)}, u32[]{:S(2)}, u32[]{:S(2)}) %all-to-all-start.1) | async-done | bytes 16777248 | tf_op jit(solution)/shard_map/all_to_all | solution.py:121
  356.3 17.7 %copy.160 = f32[2,8,128,1,16,128]{2,1,0,5,4,3:T(8,128)} copy(f32[2,8,128,1,16,128]{5,2,0,4,1,3:T(8,128)} %bitcast.18) | data formatting | bytes 33554432 | tf_op jit(solution)/shard_map/transpose | solution.py:126
  374.0 18.4 %reshape.1454 = f32[2048,2048]{0,1:T(8,128)} reshape(f32[2,8,128,1,16,128]{2,1,0,5,4,3:T(8,128)} %copy.160) | data formatting | bytes 33554432 | tf_op jit(solution)/shard_map/reshape | solution.py:127
  394.3 11.7 cholesky.254
  407.4 9.8 custom-call.20
  417.5 7.8 scatter.156
  431.7 11.9 cholesky.265
  445.6 9.8 custom-call.21
  462.2 11.7 cholesky.276
  476.0 10.0 custom-call.22
  493.7 11.7 cholesky.287
  507.4 9.8 custom-call.23
  525.9 11.7 cholesky.298
  539.7 9.8 custom-call.24
  552.0 5.9 fusion.56
  558.1 11.7 cholesky.309
  571.8 9.8 custom-call.25
  584.0 6.7 fusion.53
  590.9 11.7 cholesky.320
  604.6 9.8 custom-call.26
  616.7 6.6 fusion.50
  623.4 12.1 cholesky.331
  637.6 9.8 custom-call.27
  649.5 6.9 fusion.84
  656.6 11.9 cholesky.342
  670.4 9.8 custom-call.28
  682.3 6.3 fusion.128
  688.7 11.9 cholesky.353
  702.7 9.8 custom-call.29
  714.4 6.4 fusion.131
  720.9 11.7 cholesky.364
  734.7 10.2 custom-call.30
  746.6 5.9 fusion.134
  752.6 11.7 cholesky.375
  766.3 9.8 custom-call.31
  777.7 5.6 fusion.137
  783.5 11.7 cholesky.386
  797.2 9.8 custom-call.32
  813.1 11.9 cholesky.397
  827.1 9.8 custom-call.33
  842.1 11.7 cholesky.408
  855.8 10.2 custom-call.34
  870.0 11.7 cholesky.419
  883.8 9.8 custom-call.35
  926.9 6.2 fusion.81
  934.4 7.5 fusion.116
  943.3 8.1 fusion.87
  952.7 8.9 fusion.119
  963.0 9.8 fusion.96
  974.1 11.1 fusion.122
  986.6 11.5 fusion.72
  999.4 12.6 fusion.75
  1013.4 13.4 fusion.125
  1028.2 14.3 %fusion.78 = f32[1024,128]{1,0:T(8,128)S(1)} fusion(f32[1024,2048]{0,1:T(8,128)S(1)} %fusion.99, f32[2048,2048]{1,0:T(8,128)} %get-tuple-element.575, f32[1280,2048]{1,0:T(8,128)S(1)} %copy-done.4), kind=kOutput, calls=%fused_computation.84 | convolution fusion | flops 3020029952 | bytes 9895936 | tf_op jit(solution)/shard_map/dot_general | solution.py:53
  1046.4 6.5 pad_maximum_fusion
  1052.9 13.3 reshape.1458
  1066.1 21.0 %fusion.10 = f32[5,128,2048]{1,0,2:T(8,128)} fusion(pred[]{:T(512)S(6)} %eq.132, f32[5,2,128,2048]{2,1,0,3:T(2,128)} %reshape.1458, s32[]{:T(128)S(6)} %select_n.110), kind=kLoop, calls=%fused_computation.14 | loop fusion | flops 1310720 | bytes 10485765 | tf_op jit(solution)/shard_map/jit(_where)/select_n | solution.py:11
  1087.1 7.2 copy.230
  1103.1 221.5 %all-reduce.4.cloned.1.call-done = f32[640,2048]{0,1:T(8,128)} async-done(((f32[640,2048]{0,1:T(8,128)}), f32[640,2048]{0,1:T(8,128)}) %all-reduce.4.cloned.1.call-update) | async-done | bytes 5242896 | tf_op jit(solution)/shard_map/psum | solution.py:12
  1324.6 31.4 %fusion.33 = f32[1280,640]{1,0:T(8,128)} fusion(f32[1280,640]{1,0:T(8,128)} %copy-done.5, f32[640,2048]{0,1:T(8,128)} %all-reduce.4.cloned.1.call-done, pred[640]{0:T(1024)(128)(4,1)S(1)} %fusion.278, pred[1280]{0:T(1024)(128)(4,1)S(1)} %fusion.274, f32[1024,2048]{0,1:T(8,128)} %copy-done, f32[256,2048]{0,1:T(8,128)S(1)} %copy-done.3), kind=kOutput, calls=%fused_computation.39 | convolution fusion | flops 20137738240 | bytes 22284160 | tf_op jit(solution)/shard_map/dot_general | solution.py:141
  (211 shorter events, 189.6 us)
Async XLA Ops:
  7.2 10.8 copy-start.7
  11.9 64.8 %all-to-all-start = ((f32[2,8,128,512]{3,2,0,1:T(8,128)}), f32[2,8,128,512]{3,2,0,1:T(8,128)}, u32[]{:S(2)}, u32[]{:S(2)}) async-start(f32[2,8,128,512]{3,2,0,1:T(8,128)} %copy.155), calls=%async_computation | async-start | bytes 8388608 | tf_op jit(solution)/shard_map/all_to_all | solution.py:83
  89.3 9.7 copy-start.6
  100.9 23.7 %copy-start.5 = (f32[1280,640]{1,0:T(8,128)}, f32[1280,640]{1,0:T(8,128)S(1)}, u32[]{:S(2)}) copy-start(f32[1280,640]{1,0:T(8,128)S(1)} %bitcast_add_fusion) | copy-start | bytes 9830404
  108.7 247.6 %all-to-all-start.1 = ((f32[128,256,128]{2,1,0:T(8,128)}), f32[128,256,128]{2,1,0:T(8,128)}, u32[]{:S(2)}, u32[]{:S(2)}) async-start(f32[128,256,128]{2,1,0:T(8,128)} %stack.2), calls=%async_computation.1 | async-start | bytes 33554432 | tf_op jit(solution)/shard_map/all_to_all | solution.py:121
  119.0 778.8 %all-gather.2.cloned.1.call-start = ((), (), s32[]{:S(2)}) async-start(), calls=%async_computation.2 | async-start | bytes 11141120 | tf_op jit(solution)/shard_map/all_gather | solution.py:113
  125.5 1199.1 %all-reduce.4.cloned.1.call-start = ((), (), s32[]{:S(2)}) async-start(), calls=%async_computation.3 | async-start | bytes 10485760 | tf_op jit(solution)/shard_map/psum | solution.py:12
  895.3 2.5 copy-start.1
  897.8 6.8 copy-start.4
  1043.1 3.3 copy-start
  1087.1 7.2 copy-start.2
  1097.8 226.8 %copy-start.3 = (f32[256,2048]{0,1:T(8,128)S(1)}, f32[256,2048]{0,1:T(8,128)}, u32[]{:S(2)}) copy-start(f32[256,2048]{0,1:T(8,128)} %copy.215) | copy-start | bytes 6291460
Sparse Core Ops, SparseCore 0:
  125.6 269.2 all-gather.1
  1094.4 230.1 all-reduce.3
